TPU v7x, 128 devices: a whole 4x4x4 slice. The times are simulated.
128 devices in a mesh: group: 2 (over core), dev: 64 (over z, x, y).
Axes of the slice: x: 4, y: 4, z: 4, core: 2. Of those that a mesh axis runs over, the one named last changes fastest.
Arguments:
- tokens: bfloat16 [2048, 7168], P('dev', 'group'), may hold values from -6 to 6
- routes: int32 [2048, 8], P('dev'), may hold values from 0 to 63, all different within a row; in each aligned block of 32 rows (0 to 31, 32 to 63, ...) at most 10 rows name the same one
- route_weights: float32 [2048, 8], P('dev'), may hold values from 0.05 to 0.6
- placement: int32 [64], replicated, may hold values from 0 to 63, each once
- w_gate: bfloat16 [64, 7168, 1024], P('dev', None, 'group'), may hold values from -0.0625 to 0.0625
- w_up: bfloat16 [64, 7168, 1024], P('dev', None, 'group'), may hold values from -0.0625 to 0.0625
- w_down: bfloat16 [64, 1024, 7168], P('dev', 'group'), may hold values from -0.1875 to 0.1875
Outputs:
- expert_mix: bfloat16 [2048, 7168], P('dev', 'group')
Inputs may be any that keep to these rules, and one draw needn't show every extreme that they name: `routes`: in the rows of one device (aligned blocks of 32 rows) no expert is named by more than 10 rows; a row names 8 different experts. `placement`: a permutation: every slot holds one expert.
All inputs are finite; a program needn't handle non-finite values.
Results may differ from a plain program's by a relative error of at most 0.025.
Values may be sent and summed in bfloat16 or wider, within the bound.
A program may use at most 192 MiB of HBM per device.

v0:
```python
import jax
import jax.numpy as jnp
from jax import lax
from jax.sharding import PartitionSpec as P


def body(tokens, routes, route_weights, placement, w_gate, w_up, w_down):
    local_tokens, chosen = routes.shape
    experts = placement.shape[0]
    half_width = tokens.shape[1]
    capacity = min(5 * local_tokens * chosen // (2 * experts), local_tokens)
    flat_routes = routes.reshape(-1)
    onehot = (flat_routes[:, None] == jnp.arange(experts, dtype=jnp.int32)[None, :]).astype(
        jnp.int32
    )
    position = jnp.sum(jnp.cumsum(onehot, axis=0) * onehot, axis=1) - 1
    destination = jnp.sum(onehot * placement[None, :], axis=1)
    slot_index = destination * capacity + position
    owner = jnp.arange(local_tokens * chosen, dtype=jnp.int32) // chosen
    outgoing = (
        jnp.zeros((experts * capacity, half_width), dtype=jnp.bfloat16)
        .at[slot_index]
        .set(tokens[owner])
    )
    received = lax.all_to_all(
        outgoing.reshape(experts, capacity, half_width),
        "dev",
        split_axis=0,
        concat_axis=0,
        tiled=True,
    )
    token_rows = received.reshape(experts * capacity, half_width)
    gate_weight = w_gate[0]
    up_weight = w_up[0]
    full_rows = lax.all_gather(token_rows, "group", axis=1, tiled=True)
    gate = jnp.dot(full_rows, gate_weight, preferred_element_type=jnp.float32)
    upper = jnp.dot(full_rows, up_weight, preferred_element_type=jnp.float32)
    hidden = (jax.nn.silu(gate) * upper).astype(jnp.bfloat16)
    section = jnp.dot(hidden, w_down[0], preferred_element_type=jnp.float32).astype(jnp.bfloat16)
    mixing = route_weights.reshape(-1)[:, None]
    widened = lax.optimization_barrier(section).astype(jnp.float32)
    summed = lax.psum_scatter(
        widened.astype(jnp.bfloat16), "group", scatter_dimension=1, tiled=True
    ).astype(jnp.float32)
    returned = lax.all_to_all(
        summed.reshape(experts, capacity, half_width).astype(jnp.bfloat16),
        "dev",
        split_axis=0,
        concat_axis=0,
        tiled=True,
    ).astype(jnp.float32)
    picked = returned.reshape(experts * capacity, half_width)[slot_index]
    expert_mix = jnp.sum(
        (picked * mixing).reshape(local_tokens, chosen, half_width), axis=1
    ).astype(jnp.bfloat16)
    return expert_mix


def solution(mesh):
    in_specs = (
        P("dev", "group"),
        P("dev", None),
        P("dev", None),
        P(),
        P("dev", None, "group"),
        P("dev", None, "group"),
        P("dev", "group", None),
    )
    out_specs = P("dev", "group")
    return jax.shard_map(body, mesh=mesh, in_specs=in_specs, out_specs=out_specs, check_vma=False)
```

profile of v0, /device:TPU:1, one launch (start us, length us, event | category | flops | bytes accessed | tf_op | source)
XLA Modules:
  0.0 350.4 jit_solution(18157160439944555771)
XLA Ops:
  6.5 0.8 copy.9
  7.3 0.1 eq.29
  7.4 0.1 eq.25
  7.6 0.6 reduce-window.6
  8.2 0.2 slice_reduce_fusion
  8.4 0.8 select_reduce_fusion
  9.2 11.4 %scatter_custom_fusion = bf16[640,3584]{1,0:T(8,128)(2,1)} fusion(s32[256]{0:T(256)S(1)} %bitcast.38, bf16[]{:T(256)} %constant.29.clone.1, bf16[32,3584]{1,0:T(8,128)(2,1)S(1)} %copy-done, s32[1024]{0:T(1024)S(1)} %pad_clamp_fusion.1), kind=kCustom, calls=%fused_computation.11 | custom fusion | bytes 4587522 | tf_op jit(solution)/shard_map/scatter | solution.py:23
  20.6 7.7 %reshape.115 = bf16[64,10,3584]{2,1,0:T(8,128)(2,1)} reshape(bf16[640,3584]{1,0:T(8,128)(2,1)} %scatter_custom_fusion) | data formatting | bytes 9175040 | tf_op jit(solution)/shard_map/reshape | solution.py:26
  28.3 96.6 %all_to_all.10 = bf16[64,10,3584]{2,1,0:T(8,128)(2,1)} all-to-all(bf16[64,10,3584]{2,1,0:T(8,128)(2,1)} %reshape.115), channel_id=1, replica_groups=mesh['group'=2,'dev'=64] {'dev'}, dimensions={0} | all-to-all | bytes 9175040 | tf_op jit(solution)/shard_map/all_to_all | solution.py:25
  125.0 7.9 %reshape.116 = bf16[640,3584]{1,0:T(8,128)(2,1)} reshape(bf16[64,10,3584]{2,1,0:T(8,128)(2,1)} %all_to_all.10) | data formatting | bytes 9175040 | tf_op jit(solution)/shard_map/reshape | solution.py:32
  133.0 0.0 reduce-scatter.2.cloned.1.call-start
  133.0 24.5 %all-gather.2.cloned.1.call-done = bf16[640,7168]{1,0:T(8,128)(2,1)} async-done(((bf16[640,3584]{1,0:T(8,128)(2,1)}), bf16[640,7168]{1,0:T(8,128)(2,1)}) %all-gather.2.cloned.1.call-update) | async-done | bytes 9175056 | tf_op jit(solution)/shard_map/all_gather | solution.py:35
  157.5 9.7 %fusion.3 = f32[640,512]{1,0:T(8,128)S(1)} fusion(bf16[640,7168]{1,0:T(8,128)(2,1)} %all-gather.2.cloned.1.call-done, bf16[1,7168,512]{2,1,0:T(8,128)(2,1)} %param.11), kind=kOutput, calls=%fused_computation.7 | convolution fusion | flops 4697620480 | bytes 17825792 | tf_op jit(solution)/shard_map/dot_general | solution.py:36
  167.2 8.2 %fusion.12 = bf16[640,512]{1,0:T(8,128)(2,1)S(1)} fusion(bf16[640,7168]{1,0:T(8,128)(2,1)S(1)} %copy-done.3, bf16[1,7168,512]{2,1,0:T(8,128)(2,1)} %param.12, f32[640,512]{1,0:T(8,128)S(1)} %fusion.3), kind=kOutput, calls=%fused_computation.15 | convolution fusion | flops 4699586560 | bytes 18481152 | tf_op jit(solution)/shard_map/dot_general | solution.py:37
  175.5 7.3 %convolution_convert_fusion = bf16[640,7168]{1,0:T(8,128)(2,1)} fusion(bf16[640,512]{1,0:T(8,128)(2,1)S(1)} %fusion.12, bf16[1,512,7168]{2,1,0:T(8,128)(2,1)S(1)} %bitcast.43), kind=kOutput, calls=%fused_computation.3 | convolution fusion | flops 4702208000 | bytes 17170432 | tf_op jit(solution)/shard_map/dot_general | solution.py:39
  182.8 0.0 reduce-scatter.2.cloned.1.call-update
  182.8 21.7 %reduce-scatter.2.cloned.1.call-done = bf16[640,3584]{1,0:T(8,128)(2,1)} async-done(((bf16[640,7168]{1,0:T(8,128)(2,1)}), bf16[640,3584]{1,0:T(8,128)(2,1)}) %reduce-scatter.2.cloned.1.call-update) | async-done | bytes 4587536 | tf_op jit(solution)/shard_map/reduce_scatter | solution.py:42
  204.5 7.7 %convert_element_type.25 = bf16[64,10,3584]{2,1,0:T(8,128)(2,1)} reshape(bf16[640,3584]{1,0:T(8,128)(2,1)} %reduce-scatter.2.cloned.1.call-done) | data formatting | bytes 9175040 | tf_op jit(solution)/shard_map/convert_element_type | solution.py:46
  212.2 10.7 %all-to-all-start.1 = ((bf16[64,10,3584]{2,1,0:T(8,128)(2,1)}), bf16[64,10,3584]{2,1,0:T(8,128)(2,1)}, u32[]{:S(2)}, u32[]{:S(2)}) async-start(bf16[64,10,3584]{2,1,0:T(8,128)(2,1)} %convert_element_type.25), calls=%async_computation.2 | async-start | bytes 14680064 | tf_op jit(solution)/shard_map/all_to_all | solution.py:45
  222.9 0.1 copy.12
  223.0 98.7 %all-to-all-done.1 = bf16[64,10,3584]{2,1,0:T(8,128)(2,1)} async-done(((bf16[64,10,3584]{2,1,0:T(8,128)(2,1)}), bf16[64,10,3584]{2,1,0:T(8,128)(2,1)}, u32[]{:S(2)}, u32[]{:S(2)}) %all-to-all-start.1) | async-done | bytes 4587552 | tf_op jit(solution)/shard_map/all_to_all | solution.py:45
  321.7 9.1 %reshape.120 = f32[640,3584]{1,0:T(8,128)} reshape(bf16[64,10,3584]{2,1,0:T(8,128)(2,1)} %all-to-all-done.1) | data formatting | bytes 13762560 | tf_op jit(solution)/shard_map/reshape | solution.py:52
  330.9 8.8 %gather_fusion = f32[256,3584]{1,0:T(8,128)} fusion(f32[640,3584]{1,0:T(8,128)} %reshape.120, s32[1024]{0:T(1024)S(1)} %pad_clamp_fusion), kind=kCustom, calls=%fused_computation.1 | custom fusion | bytes 7341056 | tf_op jit(solution)/shard_map/gather | solution.py:52
  339.7 3.9 %fusion.5 = bf16[32,3584]{1,0:T(8,128)(2,1)} fusion(f32[256,3584]{1,0:T(8,128)} %gather_fusion, f32[32,8]{1,0:T(8,128)S(1)} %copy.12), kind=kLoop, calls=%fused_computation.10 | loop fusion | flops 1720320 | bytes 3900416 | tf_op jit(solution)/shard_map/reduce_sum | solution.py:53
  (23 shorter events, 0.1 us)
Async XLA Ops:
  6.5 2.7 copy-start
  6.5 150.9 %all-gather.2.cloned.1.call-start = ((), (), s32[]{:S(2)}) async-start(), calls=%async_computation.3 | async-start | bytes 13762560 | tf_op jit(solution)/shard_map/all_gather | solution.py:35
  133.0 71.5 %reduce-scatter.2.cloned.1.call-start = ((), (), s32[]{:S(2)}) async-start(), calls=%async_computation.4 | async-start | bytes 13762560 | tf_op jit(solution)/shard_map/reduce_scatter | solution.py:42
  157.5 9.7 %copy-start.3 = (bf16[640,7168]{1,0:T(8,128)(2,1)S(1)}, bf16[640,7168]{1,0:T(8,128)(2,1)}, u32[]{:S(2)}) copy-start(bf16[640,7168]{1,0:T(8,128)(2,1)} %all-gather.2.cloned.1.call-done) | copy-start | bytes 27525124
  157.5 18.0 %slice-start = ((s8[7340032]{0:T(1024)(128)(4,1)}), s8[4194304]{0:T(1024)(128)(4,1)S(1)}, s32[]{:S(2)}) async-start(s8[7340032]{0:T(1024)(128)(4,1)} %bitcast.42), calls=%async_computation.5 | async-start | bytes 8388608
  167.2 8.3 %slice-start.1 = ((s8[7340032]{0:T(1024)(128)(4,1)}), s8[3145728]{0:T(1024)(128)(4,1)S(1)}, s32[]{:S(2)}) async-start(s8[7340032]{0:T(1024)(128)(4,1)} %bitcast.42), calls=%async_computation.6 | async-start | bytes 6291456
  212.2 10.7 %copy-start.2 = (f32[32,8]{0,1:T(8,128)S(1)}, f32[32,8]{0,1:T(8,128)}, u32[]{:S(2)}) copy-start(f32[32,8]{0,1:T(8,128)} %param.9) | copy-start | bytes 3076
  212.2 109.6 %all-to-all-start.1 = ((bf16[64,10,3584]{2,1,0:T(8,128)(2,1)}), bf16[64,10,3584]{2,1,0:T(8,128)(2,1)}, u32[]{:S(2)}, u32[]{:S(2)}) async-start(bf16[64,10,3584]{2,1,0:T(8,128)(2,1)} %convert_element_type.25), calls=%async_computation.2 | async-start | bytes 14680064 | tf_op jit(solution)/shard_map/all_to_all | solution.py:45
  330.9 12.7 %copy-start.1 = (bf16[32,3584]{1,0:T(8,128)(2,1)S(1)}, bf16[32,3584]{1,0:T(8,128)(2,1)}, u32[]{:S(2)}) copy-start(bf16[32,3584]{1,0:T(8,128)(2,1)} %param.7) | copy-start | bytes 688132
Sparse Core Ops, SparseCore 0:
  133.1 24.3 all-gather.1
  182.9 21.4 reduce-scatter.1
where the time goes:
time: 357 us; the launch traced here: 350 us
  waiting for transfers between devices  145 us (41%)
  blocking collectives  96.6 us (27%)
  local copies, waits for them, and re-layouts  54 us (15%)
  matrix products  25.2 us (7%)
  between operations  13.5 us (4%)
  starting transfers between devices  10.8 us (3%)
  other arithmetic  5.38 us (2%)
    all_to_all x1, waiting for transfers between devices, body(): lax.all_to_all(summed.reshape(experts, capacity, half_width).astype(jnp.b...  98.7 us
    all_to_all x1, blocking collectives, body(): lax.all_to_all(outgoing.reshape(experts, capacity, half_width), 'dev', sp...  96.6 us
    all_gather x1, waiting for transfers between devices, body(): full_rows = lax.all_gather(token_rows, 'group', axis=1, tiled=True)  24.5 us
    reduce_scatter x1, waiting for transfers between devices, body(): lax.psum_scatter(widened.astype(jnp.bfloat16), 'group', scatter_dimension...  21.7 us
    scatter x1, local copies, waits for them, and re-layouts, body(): outgoing = jnp.zeros((experts * capacity, half_width), dtype=jnp.bfloat16...  11.4 us
    all_to_all x1, starting transfers between devices, body(): lax.all_to_all(summed.reshape(experts, capacity, half_width).astype(jnp.b...  10.7 us
    dot_general x1, matrix products, body(): gate = jnp.dot(full_rows, gate_weight, preferred_element_type=jnp.float32)  9.68 us
    reshape x1, local copies, waits for them, and re-layouts, body(): picked = returned.reshape(experts * capacity, half_width)[slot_index]  9.13 us
  transfers between devices with their start and end apart: 3, of which 3 were waited for; matrix products, arithmetic and copies ran while one was open for 0% of the time, Pallas kernels for 0%

commit v1 on v0

v1 whole, which is shorter than its diff:
```python
import jax
import jax.numpy as jnp
import numpy as np
from jax import lax
from jax.experimental import pallas as pl
from jax.experimental.pallas import tpu as pltpu
from jax.sharding import PartitionSpec as P

MESH = pl.DeviceIdType.MESH
BF = jnp.bfloat16
F32 = jnp.float32
CW = 512
MAIN, REST = 8, 2
A_AG, B_AG, C_OUT, C_BACK, B_RS, A_RS = range(6)


def rest_matrices():
    mats = np.zeros((6, 128, 128), np.float32)
    for rho in range(3):
        for q in np.ndindex(4, 4, 4):
            for j in range(REST):

                def row(turn):
                    a, b, c = q[turn], q[(turn + 2) % 3], q[(turn + 1) % 3]
                    return ((b // 2) * 4 + c) * 16 + ((b % 2) * 4 + a) * 2 + j

                mats[rho, row(0), row(rho)] = 1
        mats[3 + rho] = mats[rho].T
    return mats


def main_row(q, rho):
    a, b, c = q[rho], q[(rho + 2) % 3], q[(rho + 1) % 3]
    return ((b // 2) * 4 + c) * 80 + ((b % 2) * 4 + a) * MAIN


def dot(x, y):
    return jnp.dot(x, y, preferred_element_type=F32)


def kernel(
    tok, info, perm, wg_hbm, wu_hbm, wd_hbm, out,
    WG, WU, WD, B, SB, X, XP, acc, HR, RB, RSB, RA, QB, IB, SEL, WT,
    ss, rs, iss, irs, ess, ers, hss, hrs, wsem, dss, drs,
):
    g = lax.axis_index("group")
    dev = lax.axis_index("dev")
    n = B.shape[0]
    half = n * CW

    def stride(ax):
        return lax.div(32 - 33 * ax + 9 * ax * ax, 2)

    def coord(ax):
        return lax.rem(lax.div(dev, stride(ax)), 4)

    def peer(ax, k):
        at = coord(ax)
        return dev + (lax.rem(at + k, 4) - at) * stride(ax)

    def axes(slot, core):
        rho = lax.rem(slot + core, 3)
        return rho, lax.rem(rho + 2, 3), lax.rem(rho + 1, 3)

    def remote(src, dst, s, r, ax, k):
        return pltpu.make_async_remote_copy(
            src, dst, s, r, device_id={"dev": peer(ax, k)}, device_id_type=MESH
        )

    def across(src, dst, s, r):
        return pltpu.make_async_remote_copy(
            src, dst, s, r, device_id={"group": 1 - g}, device_id_type=MESH
        )

    def block(i, size):
        return pl.ds(pl.multiple_of(i * size, size), size)

    def a_ag(i, k):
        a, b, c = axes(lax.rem(i, 3), g)
        here = B.at[i, block(coord(b) * 4 + coord(a), 32)]
        return remote(tok.at[:, block(i, CW)], here, ss.at[A_AG, i, k - 1], rs.at[A_AG, i, k - 1], a, k)

    def b_ag(i, k):
        a, b, c = axes(lax.rem(i, 3), g)
        here = B.at[i, block(coord(b), 128)]
        return remote(here, here, ss.at[B_AG, i, k - 1], rs.at[B_AG, i, k - 1], b, k)

    def c_out(i, k):
        a, b, c = axes(lax.rem(i, 3), g)
        to = lax.rem(coord(c) + k, 4)
        return remote(SB.at[i, :, to], X.at[i, :, coord(c)], ss.at[C_OUT, i, k - 1], rs.at[C_OUT, i, k - 1], c, k)

    def c_back(i, k):
        a, b, c = axes(lax.rem(i, 3), g)
        to = lax.rem(coord(c) + k, 4)
        return remote(SB.at[i, :, to], RB.at[i, :, coord(c)], ss.at[C_BACK, i, k - 1], rs.at[C_BACK, i, k - 1], c, k)

    def b_rs(i, k):
        a, b, c = axes(lax.rem(i, 3), g)
        to = lax.rem(coord(b) + k, 4)
        return remote(B.at[i, block(to, 128)], RSB.at[i, k - 1], ss.at[B_RS, i, k - 1], rs.at[B_RS, i, k - 1], b, k)

    def a_rs(i, k):
        a, b, c = axes(lax.rem(i, 3), g)
        to = lax.rem(coord(a) + k, 4)
        return remote(QB.at[i, block(to, 32)], RA.at[i, k - 1], ss.at[A_RS, i, k - 1], rs.at[A_RS, i, k - 1], a, k)

    def info_a(r, k):
        a, b, c = axes(r, g)
        return remote(info, IB.at[r, coord(b), coord(a)], iss.at[0, r, k - 1], irs.at[0, r, k - 1], a, k)

    def info_b(r, k):
        a, b, c = axes(r, g)
        here = IB.at[r, coord(b)]
        return remote(here, here, iss.at[1, r, k - 1], irs.at[1, r, k - 1], b, k)

    def rows_across(i):
        return across(X.at[i], XP.at[i], ess.at[i], ers.at[i])

    def hidden_across(rho):
        return across(HR.at[rho, g], HR.at[rho, g], hss.at[rho], hrs.at[rho])

    def every(fn):
        def step(i, carry):
            fn(i)
            return carry

        lax.fori_loop(0, n, step, 0)

    bar = pltpu.get_barrier_semaphore()
    for ax in range(3):
        for k in (1, 2, 3):
            pl.semaphore_signal(bar, inc=1, device_id={"dev": peer(ax, k)}, device_id_type=MESH)
    pl.semaphore_signal(bar, inc=1, device_id={"group": 1 - g}, device_id_type=MESH)
    pl.semaphore_wait(bar, 10)

    for r in range(3):
        a, b, c = axes(r, g)
        for k in (1, 2, 3):
            info_a(r, k).start()
        IB[r, coord(b), coord(a)] = info[...]

    @every
    def _(i):
        a, b, c = axes(lax.rem(i, 3), g)
        for k in (1, 2, 3):
            a_ag(i, k).start()
        B[i, block(coord(b) * 4 + coord(a), 32), :] = tok[:, block(i, CW)]

    wg_copy = pltpu.make_async_copy(wg_hbm.at[0], WG, wsem.at[0])
    wu_copy = pltpu.make_async_copy(wu_hbm.at[0], WU, wsem.at[1])
    hid = WG.shape[1]
    wd_copy = pltpu.make_async_copy(wd_hbm.at[0, :, block(g, half)], WD.at[block(g, hid)], wsem.at[2])
    wd_across = across(wd_hbm.at[0, :, block(1 - g, half)], WD.at[block(g, hid)], dss, drs)
    wg_copy.start()
    wu_copy.start()
    wd_copy.start()
    wd_across.start()

    for r in range(3):
        for k in (1, 2, 3):
            info_a(r, k).wait_recv()
        for k in (1, 2, 3):
            info_b(r, k).start()

    @every
    def _(i):
        for k in (1, 2, 3):
            a_ag(i, k).wait_recv()
        for k in (1, 2, 3):
            b_ag(i, k).start()

    acc[...] = jnp.zeros_like(acc)

    lane = lax.broadcasted_iota(jnp.int32, (8, 128), 1)
    seg_mask = [(lane >= 32 * a) & (lane < 32 * a + 32) for a in range(4)]
    lane1 = lax.broadcasted_iota(jnp.int32, (16, 128), 1)
    seg16 = sum(jnp.where(lane1 >= 32 * a, 1, 0) for a in (1, 2, 3))
    row1 = lax.broadcasted_iota(jnp.int32, (16, 128), 0)
    odd_b = jnp.where(((row1 >= 4) & (row1 < 8)) | (row1 >= 12), 1, 0)
    src8 = (odd_b * 4 + seg16).astype(F32)
    ti = lax.broadcasted_iota(jnp.int32, (128, 128), 0)
    tj = lax.broadcasted_iota(jnp.int32, (128, 128), 1)
    start_j = sum(jnp.where(tj >= 32 * a, 32, 0) for a in (1, 2, 3))
    before = jnp.where((ti < tj) & (ti >= start_j), 1.0, 0.0).astype(BF)
    iota_q = lax.broadcasted_iota(jnp.int32, (80, 128), 0).astype(F32)
    iota_k = lax.broadcasted_iota(jnp.int32, (128, 320), 1).astype(F32)

    for r in range(3):
        a_ax, b_ax, c_ax = axes(r, g)
        for k in (1, 2, 3):
            info_b(r, k).wait_recv()
        hits, weights = [], []
        for b in range(4):
            dest = sum(jnp.where(seg_mask[a], IB[r, b, a, 0:8, :], 0.0) for a in range(4))
            wts = sum(jnp.where(seg_mask[a], IB[r, b, a, 8:16, :], 0.0) for a in range(4))
            for d in range(4):
                target = (dev + (d - coord(c_ax)) * stride(c_ax)).astype(F32)
                hit = dest == target
                hits.append(jnp.sum(jnp.where(hit, 1.0, 0.0), axis=0, keepdims=True))
                weights.append(jnp.sum(jnp.where(hit, wts, 0.0), axis=0, keepdims=True))
        hits = jnp.concatenate(hits, axis=0)
        weights = jnp.concatenate(weights, axis=0)
        rank = dot(hits.astype(BF), before)
        place = jnp.where(rank < MAIN, src8 * MAIN + rank, 64 + src8 * REST + (rank - MAIN))
        place = jnp.where(hits > 0, place, -1000.0)
        fill = jnp.zeros((112, 128), F32)
        place_t = jnp.transpose(jnp.concatenate([place, fill], axis=0))
        weights_t = jnp.transpose(jnp.concatenate([weights, fill], axis=0))
        for b in range(4):
            total = jnp.zeros((128, 320), F32)
            for d in range(4):
                at = b * 4 + d
                SEL[r, b // 2, d * 80 : d * 80 + 80, (b % 2) * 128 : (b % 2) * 128 + 128] = jnp.where(
                    iota_q == place[at : at + 1, :], 1.0, 0.0
                ).astype(BF)
                total = total + jnp.where(
                    iota_k == place_t[:, at : at + 1] + 80.0 * d, weights_t[:, at : at + 1], 0.0
                )
            high = total.astype(BF)
            low = (total - high.astype(F32)).astype(BF)
            WT[0, r, b // 2, (b % 2) * 128 : (b % 2) * 128 + 128, :] = high
            WT[1, r, b // 2, (b % 2) * 128 : (b % 2) * 128 + 128, :] = low

    @every
    def _(i):
        r = lax.rem(i, 3)
        a, b, c = axes(r, g)
        for k in (1, 2, 3):
            b_ag(i, k).wait_recv()
        for h in range(2):
            picked = dot(SEL[r, h], B[i, h * 256 : h * 256 + 256, :]).astype(BF)
            SB[i, h] = picked.reshape(4, 80, CW)
        for k in (1, 2, 3):
            c_out(i, k).start()
        X[i, :, coord(c)] = SB[i, :, coord(c)]

    wg_copy.wait()
    wu_copy.wait()

    def multiply(rows_ref, i, core):
        rho, _, _ = axes(lax.rem(i, 3), core)
        rows = rows_ref[i].reshape(640, CW)
        depth = pl.ds(pl.multiple_of(core * half + i * CW, CW), CW)
        for w, weight in enumerate((WG, WU)):
            for part in range(2):
                cols = slice(part * 256, part * 256 + 256)
                acc[w, rho, :, cols] += dot(rows, weight[depth, cols])

    @every
    def _(i):
        rho, _, _ = axes(lax.rem(i, 3), g)
        for k in (1, 2, 3):
            c_out(i, k).wait_recv()
        rest = jnp.concatenate([X[i, h, c, 64:80, :] for h in range(2) for c in range(4)], axis=0)
        rest = dot(perm[rho], rest).astype(BF)
        for h in range(2):
            for c in range(4):
                at = (h * 4 + c) * 16
                X[i, h, c, 64:80, :] = rest[at : at + 16, :]
        rows_across(i).start()
        multiply(X, i, g)
        rows_across(i).wait_recv()
        multiply(XP, i, 1 - g)

    def swiglu(gate, up):
        return gate / (1.0 + jnp.exp(-gate)) * up

    for q in np.ndindex(4, 4, 4):
        rows = [slice(main_row(q, rho), main_row(q, rho) + MAIN) for rho in range(3)]
        gate = acc[0, 0, rows[0], :] + acc[0, 1, rows[1], :] + acc[0, 2, rows[2], :]
        up = acc[1, 0, rows[0], :] + acc[1, 1, rows[1], :] + acc[1, 2, rows[2], :]
        acc[0, 0, rows[0], :] = swiglu(gate, up)
    for m in range(8):
        rows = slice(m * 80 + 64, m * 80 + 80)
        gate = acc[0, 0, rows, :] + acc[0, 1, rows, :] + acc[0, 2, rows, :]
        up = acc[1, 0, rows, :] + acc[1, 1, rows, :] + acc[1, 2, rows, :]
        acc[0, 0, rows, :] = swiglu(gate, up)

    rest = jnp.concatenate([acc[0, 0, m * 80 + 64 : m * 80 + 80, :] for m in range(8)], axis=0).astype(BF)
    for rho in range(3):
        for q in np.ndindex(4, 4, 4):
            if q[rho] % 2:
                continue
            two = list(q)
            two[rho] += 1
            here = main_row(q, rho)
            one, other = main_row(q, 0), main_row(two, 0)
            HR[rho, g, here : here + 16, :] = jnp.concatenate(
                [acc[0, 0, one : one + MAIN, :], acc[0, 0, other : other + MAIN, :]], axis=0
            ).astype(BF)
        turned = dot(perm[3 + rho], rest).astype(BF)
        for m in range(8):
            HR[rho, g, m * 80 + 64 : m * 80 + 80, :] = turned[m * 16 : m * 16 + 16, :]
        hidden_across(rho).start()

    wd_copy.wait()
    wd_across.wait()
    for rho in range(3):
        hidden_across(rho).wait_recv()

    @every
    def _(i):
        rho, _, c = axes(lax.rem(i, 3), g)
        for k in (1, 2, 3):
            c_out(i, k).wait_send()
        for part in range(2):
            cols = pl.ds(pl.multiple_of(i * CW + part * 256, 256), 256)
            made = dot(HR[rho, 0], WD[0:hid, cols]) + dot(HR[rho, 1], WD[hid : 2 * hid, cols])
            SB[i, :, :, :, part * 256 : part * 256 + 256] = made.astype(BF).reshape(2, 4, 80, 256)
        for k in (1, 2, 3):
            c_back(i, k).start()
        RB[i, :, coord(c)] = SB[i, :, coord(c)]

    @every
    def _(i):
        r = lax.rem(i, 3)
        for k in (1, 2, 3):
            c_back(i, k).wait_recv()
            b_ag(i, k).wait_send()
        for h in range(2):
            rows = RB[i, h].reshape(320, CW)
            B[i, h * 256 : h * 256 + 256, :] = (dot(WT[0, r, h], rows) + dot(WT[1, r, h], rows)).astype(BF)
        for k in (1, 2, 3):
            b_rs(i, k).start()

    @every
    def _(i):
        a, b, c = axes(lax.rem(i, 3), g)
        for k in (1, 2, 3):
            b_rs(i, k).wait_recv()
        total = B[i, block(coord(b), 128), :].astype(F32)
        for k in range(3):
            total = total + RSB[i, k].astype(F32)
        QB[i] = total.astype(BF)
        for k in (1, 2, 3):
            a_rs(i, k).start()

    @every
    def _(i):
        a, b, c = axes(lax.rem(i, 3), g)
        for k in (1, 2, 3):
            a_rs(i, k).wait_recv()
        total = QB[i, block(coord(a), 32), :].astype(F32)
        for k in range(3):
            total = total + RA[i, k].astype(F32)
        out[:, block(i, CW)] = total.astype(BF)

    @every
    def _(i):
        for k in (1, 2, 3):
            a_ag(i, k).wait_send()
            c_back(i, k).wait_send()
            b_rs(i, k).wait_send()
            a_rs(i, k).wait_send()
        rows_across(i).wait_send()

    for r in range(3):
        for k in (1, 2, 3):
            info_a(r, k).wait_send()
            info_b(r, k).wait_send()
        hidden_across(r).wait_send()


def body(tokens, routes, route_weights, placement, w_gate, w_up, w_down):
    local_tokens, half = tokens.shape
    experts = placement.shape[0]
    n = half // CW
    hid = w_gate.shape[2]
    onehot = routes.T[:, :, None] == jnp.arange(experts, dtype=jnp.int32)[None, None, :]
    destination = jnp.sum(jnp.where(onehot, placement[None, None, :], 0), axis=2).astype(F32)
    info = jnp.tile(jnp.concatenate([destination, route_weights.T], axis=0), (1, 4))
    perm = jnp.asarray(rest_matrices(), BF)
    vmem = pl.BlockSpec(memory_space=pltpu.VMEM)
    hbm = pl.BlockSpec(memory_space=pl.ANY)
    dma = pltpu.SemaphoreType.DMA
    return pl.pallas_call(
        kernel,
        out_shape=jax.ShapeDtypeStruct(tokens.shape, BF),
        in_specs=[vmem, vmem, vmem, hbm, hbm, hbm],
        out_specs=vmem,
        scratch_shapes=[
            pltpu.VMEM((2 * half, hid), BF),
            pltpu.VMEM((2 * half, hid), BF),
            pltpu.VMEM((2 * hid, half), BF),
            pltpu.VMEM((n, 512, CW), BF),
            pltpu.VMEM((n, 2, 4, 80, CW), BF),
            pltpu.VMEM((n, 2, 4, 80, CW), BF),
            pltpu.VMEM((n, 2, 4, 80, CW), BF),
            pltpu.VMEM((2, 3, 640, hid), F32),
            pltpu.VMEM((3, 2, 640, hid), BF),
            pltpu.VMEM((n, 2, 4, 80, CW), BF),
            pltpu.VMEM((n, 3, 128, CW), BF),
            pltpu.VMEM((n, 3, 32, CW), BF),
            pltpu.VMEM((n, 128, CW), BF),
            pltpu.VMEM((3, 4, 4, 16, 128), F32),
            pltpu.VMEM((3, 2, 320, 256), BF),
            pltpu.VMEM((2, 3, 2, 256, 320), BF),
            dma((6, n, 3)),
            dma((6, n, 3)),
            dma((2, 3, 3)),
            dma((2, 3, 3)),
            dma((n,)),
            dma((n,)),
            dma((3,)),
            dma((3,)),
            dma((3,)),
            dma,
            dma,
        ],
        compiler_params=pltpu.CompilerParams(
            collective_id=0, has_side_effects=True, vmem_limit_bytes=64 * 1024 * 1024 - 512 * 1024
        ),
    )(tokens, info, perm, w_gate, w_up, w_down)


def solution(mesh):
    in_specs = (
        P("dev", "group"),
        P("dev", None),
        P("dev", None),
        P(),
        P("dev", None, "group"),
        P("dev", None, "group"),
        P("dev", "group", None),
    )
    out_specs = P("dev", "group")
    return jax.shard_map(body, mesh=mesh, in_specs=in_specs, out_specs=out_specs, check_vma=False)
```

time: 357 us -> 110 us (0.31); the launches traced: 350 us -> 110 us
  waiting for transfers between devices: 145 us -> 0 us
  Pallas kernels: 0 us -> 106 us
  blocking collectives: 96.6 us -> 0 us
  local copies, waits for them, and re-layouts: 54 us -> 2.33 us
  matrix products: 25.2 us -> 0 us
  between operations: 13.5 us -> 0.02 us
  starting transfers between devices: 10.8 us -> 0 us
  other arithmetic: 5.38 us -> 1.69 us
    pallas_call x0 -> x1, Pallas kernels: none -> 106 us  [body(): pl.pallas_call(kernel, out_shape=jax.ShapeDtypeStruct(tokens.shape, BF),...]
    all_to_all x1 -> x0, waiting for transfers between devices: 98.7 us -> none  [body(): lax.all_to_all(summed.reshape(experts, capacity, half_width).astype(jnp.b...]
    all_to_all x1 -> x0, blocking collectives: 96.6 us -> none  [body(): lax.all_to_all(outgoing.reshape(experts, capacity, half_width), 'dev', sp...]
    dot_general x3 -> x0, matrix products: 25.2 us -> none  [the longest x1 9.68 us: body(): gate = jnp.dot(full_rows, gate_weight, preferred_element_type=jnp.float32)]
    reshape x3 -> x0, local copies, waits for them, and re-layouts: 24.8 us -> none  [the longest x1 9.13 us: body(): picked = returned.reshape(experts * capacity, half_width)[slot_index]]
    all_gather x1 -> x0, waiting for transfers between devices: 24.5 us -> none  [body(): full_rows = lax.all_gather(token_rows, 'group', axis=1, tiled=True)]
    reduce_scatter x1 -> x0, waiting for transfers between devices: 21.7 us -> none  [body(): lax.psum_scatter(widened.astype(jnp.bfloat16), 'group', scatter_dimension...]
    scatter x1 -> x0, local copies, waits for them, and re-layouts: 11.4 us -> none  [body(): outgoing = jnp.zeros((experts * capacity, half_width), dtype=jnp.bfloat16...]
  transfers between devices with their start and end apart: 3 -> 0, of which waited for: 3 -> 0; matrix products, arithmetic and copies ran while one was open for 0% -> 0% of each run, Pallas kernels for 0% -> 0%
where the time goes in v1:
time: 110 us
  Pallas kernels  106 us (96%)
  local copies, waits for them, and re-layouts  2.33 us (2%)
  other arithmetic  1.69 us (2%)
    pallas_call x1, Pallas kernels, body(): pl.pallas_call(kernel, out_shape=jax.ShapeDtypeStruct(tokens.shape, BF),...  106 us

profile of v1, /device:TPU:1, one launch (start us, length us, event | category | flops | bytes accessed | tf_op | source)
XLA Modules:
  0.0 110.1 jit_solution(15956065701995473437)
XLA Ops:
  0.0 1.0 select_reduce_fusion
  1.0 0.7 pad_maximum_fusion
  1.7 0.7 tile.10.info
  2.4 106.0 %shard_map.82 = bf16[32,3584]{1,0:T(8,128)(2,1)} custom-call(bf16[32,3584]{1,0:T(8,128)(2,1)} %tok.1, f32[16,128]{1,0:T(8,128)} %tile.10.info, bf16[6,128,128]{2,1,0:T(8,128)(2,1)} %constant.4.clone.perm, bf16[1,7168,512]{2,1,0:T(8,128)(2,1)} %wg_hbm.1, bf16[1,7168,512]{2,1,0:T(8,128)(2,1)} %wu_hbm.1, bf16[1,512,7168]{2,1,0:T(8,128)(2,1)} %wd_hbm.1), custom_call_target="tpu_custom_call" | custom-call | tf_op jit(solution)/shard_map/pallas_call | solution.py:377
  108.4 1.6 %copy.10 = bf16[32,3584]{1,0:T(8,128)(2,1)} copy(bf16[32,3584]{1,0:T(8,128)(2,1)} %shard_map.82) | data formatting | bytes 458752
  (2 shorter events, 0.0 us)

commit v2 on v1

v2 whole, which is shorter than its diff:
```python
import jax
import jax.numpy as jnp
import numpy as np
from jax import lax
from jax.experimental import pallas as pl
from jax.experimental.pallas import tpu as pltpu
from jax.sharding import PartitionSpec as P

MESH = pl.DeviceIdType.MESH
BF = jnp.bfloat16
F32 = jnp.float32
CW = 512
EARLY = 2
COMBINE = 3
FIRST = 5
PACE = (5, 9, 12)
MAIN, REST = 8, 2
A_AG, B_AG, B_ON, C_OUT, C_BACK, B_RS, A_RS = range(7)


def place_of(q, rho):
    a, b, c = q[rho], q[(rho + 2) % 3], q[(rho + 1) % 3]
    return sum(q) % 2, c, b * 2 + a // 2


def main_row(q, rho):
    h, c, at = place_of(q, rho)
    return (h * 4 + c) * 80 + at * MAIN


def rest_matrices():
    mats = np.zeros((2, 3, 2, 64, 64), np.float32)
    for rho in range(3):
        for q in np.ndindex(4, 4, 4):
            h, c, at = place_of(q, rho)
            _, c0, at0 = place_of(q, 0)
            for j in range(REST):
                mats[0, rho, h, c0 * 16 + at0 * 2 + j, c * 16 + at * 2 + j] = 1
    mats[1] = np.swapaxes(mats[0], -1, -2)
    return mats


def dot(x, y):
    return jnp.dot(x, y, preferred_element_type=F32)


def kernel(
    tok, routes, weights_in, placement, perm, wg_hbm, wu_hbm, wd_hbm, out,
    WG, WU, WD, B, SB, X, XP, acc, HR, RB, RSB, RA, QB, IB, SEL, WT, info,
    ss, rs, iss, irs, ess, ers, hss, hrs, wsem, dss, drs,
):
    g = lax.axis_index("group")
    dev = lax.axis_index("dev")
    n = B.shape[0]
    half = n * CW

    def stride(ax):
        return lax.div(32 - 33 * ax + 9 * ax * ax, 2)

    def coord(ax):
        return lax.rem(lax.div(dev, stride(ax)), 4)

    def peer(ax, k):
        at = coord(ax)
        return dev + (lax.rem(at + k, 4) - at) * stride(ax)

    def axes(slot, core):
        rho = lax.rem(slot + core, 3)
        return rho, lax.rem(rho + 2, 3), lax.rem(rho + 1, 3)

    def remote(src, dst, s, r, ax, k):
        return pltpu.make_async_remote_copy(
            src, dst, s, r, device_id={"dev": peer(ax, k)}, device_id_type=MESH
        )

    def across(src, dst, s, r):
        return pltpu.make_async_remote_copy(
            src, dst, s, r, device_id={"group": 1 - g}, device_id_type=MESH
        )

    def block(i, size):
        return pl.ds(pl.multiple_of(i * size, size), size)

    parity = lax.rem(coord(0) + coord(1) + coord(2), 2)

    def a_ag(i, k):
        a, b, c = axes(lax.rem(i, 3), g)
        here = B.at[i, parity, block(coord(b) * 2 + lax.div(coord(a), 2), 32)]
        sems = (A_AG, i, 0, k - 1)
        return remote(tok.at[:, block(i, CW)], here, ss.at[sems], rs.at[sems], a, k)

    def b_ag(i, h, k):
        a, b, c = axes(lax.rem(i, 3), g)
        here = B.at[i, h, block(coord(b), 64)]
        sems = (B_AG, i, h, k - 1)
        return remote(here, here, ss.at[sems], rs.at[sems], b, k)

    def b_on(i, h, k):
        a, b, c = axes(lax.rem(i, 3), g)
        here = B.at[i, h, block(lax.rem(coord(b) + 4 - k, 4) * 2 + (k - 1) // 2, 32)]
        sems = (B_ON, i, h, k - 1)
        return remote(here, here, ss.at[sems], rs.at[sems], b, k)

    def c_out(i, h, k):
        a, b, c = axes(lax.rem(i, 3), g)
        to = lax.rem(coord(c) + k, 4)
        sems = (C_OUT, i, h, k - 1)
        return remote(SB.at[i, h, to], X.at[i, h, coord(c)], ss.at[sems], rs.at[sems], c, k)

    def c_back(i, h, k):
        a, b, c = axes(lax.rem(i, 3), g)
        to = lax.rem(coord(c) + k, 4)
        sems = (C_BACK, i, h, k - 1)
        return remote(SB.at[i, h, to], RB.at[i, h, coord(c)], ss.at[sems], rs.at[sems], c, k)

    def b_rs(i, h, k):
        a, b, c = axes(lax.rem(i, 3), g)
        to = lax.rem(coord(b) + k, 4)
        sems = (B_RS, i, h, k - 1)
        return remote(B.at[i, h, block(to, 64)], RSB.at[i, h, k - 1], ss.at[sems], rs.at[sems], b, k)

    def a_rs(i, k):
        a, b, c = axes(lax.rem(i, 3), g)
        to = lax.div(lax.rem(coord(a) + k, 4), 2)
        h = parity if k == 2 else 1 - parity
        sems = (A_RS, i, 0, k - 1)
        return remote(QB.at[i, h, block(to, 32)], RA.at[i, k - 1], ss.at[sems], rs.at[sems], a, k)

    def info_a(r, k):
        a, b, c = axes(r, g)
        return remote(info, IB.at[r, coord(b), coord(a)], iss.at[0, r, k - 1], irs.at[0, r, k - 1], a, k)

    def info_b(r, k):
        a, b, c = axes(r, g)
        here = IB.at[r, coord(b)]
        return remote(here, here, iss.at[1, r, k - 1], irs.at[1, r, k - 1], b, k)

    def rows_across(i, h):
        return across(X.at[i, h], XP.at[i, h], ess.at[i, h], ers.at[i, h])

    def hidden_across(rho, h):
        part = HR.at[rho, g, pl.ds(h * 320, 320)]
        return across(part, part, hss.at[rho, h], hrs.at[rho, h])

    def in_half(h, same, other):
        pl.when(parity == h)(lambda: [fn() for fn in same] and None)
        pl.when(parity != h)(lambda: [fn() for fn in other] and None)

    def loop(start, stop, fn):
        def step(i, carry):
            fn(i)
            return carry

        lax.fori_loop(start, stop, step, 0)

    def every(fn):
        loop(0, n, fn)

    def of(fn, h):
        return lambda i: fn(i, h)

    def stages(*work):
        def step(s):
            for fn, lag, *first in work:
                start = lag + (first[0] if first else 0)
                pl.when((s >= start) & (s < n + lag))(lambda fn=fn, lag=lag: fn(s - lag))

        loop(0, n + max(w[1] for w in work), step)

    bar = pltpu.get_barrier_semaphore()
    for ax in range(3):
        for k in (1, 2, 3):
            pl.semaphore_signal(bar, inc=1, device_id={"dev": peer(ax, k)}, device_id_type=MESH)
    pl.semaphore_signal(bar, inc=1, device_id={"group": 1 - g}, device_id_type=MESH)
    dest = jnp.zeros(routes.shape, jnp.int32)
    for e in range(placement.shape[0]):
        dest = jnp.where(routes[...] == e, placement[e], dest)
    info[0:8, :] = jnp.concatenate([dest.astype(F32)] * 4, axis=1)
    info[8:16, :] = jnp.concatenate([weights_in[...]] * 4, axis=1)
    acc[...] = jnp.zeros_like(acc)
    pl.semaphore_wait(bar, 10)

    for r in range(3):
        a, b, c = axes(r, g)
        for k in (1, 2, 3):
            info_a(r, k).start()
        IB[r, coord(b), coord(a)] = info[...]

    @every
    def _(i):
        a, b, c = axes(lax.rem(i, 3), g)
        for k in (1, 2, 3):
            a_ag(i, k).start()
        B[i, parity, block(coord(b) * 2 + lax.div(coord(a), 2), 32), :] = tok[:, block(i, CW)]

    wg_copy = pltpu.make_async_copy(wg_hbm.at[0], WG, wsem.at[0])
    wu_copy = pltpu.make_async_copy(wu_hbm.at[0], WU, wsem.at[1])
    hid = WG.shape[1]
    wd_copy = pltpu.make_async_copy(wd_hbm.at[0, :, block(g, half)], WD.at[block(g, hid)], wsem.at[2])
    wd_across = across(wd_hbm.at[0, :, block(1 - g, half)], WD.at[block(g, hid)], dss, drs)
    wg_copy.start()
    wu_copy.start()
    wd_copy.start()
    wd_across.start()

    def second_axis(i, h):
        in_half(
            h,
            [lambda: a_ag(i, 2).wait_recv()],
            [lambda: a_ag(i, 1).wait_recv(), lambda: a_ag(i, 3).wait_recv()],
        )
        for k in (1, 3):
            b_ag(i, h, k).start()

    def pass_on(i, h):
        for k in (1, 3):
            b_ag(i, h, k).wait_recv()
            b_on(i, h, k).start()

    for r in range(3):
        for k in (1, 2, 3):
            info_a(r, k).wait_recv()
        for k in (1, 2, 3):
            info_b(r, k).start()

    stages((of(second_axis, 0), 0))
    stages((of(second_axis, 1), 0), (of(pass_on, 0), 0))

    lane = lax.broadcasted_iota(jnp.int32, (8, 128), 1)
    seg_mask = [(lane >= 32 * a) & (lane < 32 * a + 32) for a in range(4)]
    lane1 = lax.broadcasted_iota(jnp.int32, (16, 128), 1)
    seg16 = sum(jnp.where(lane1 >= 32 * a, 1, 0) for a in (1, 2, 3))
    row1 = lax.broadcasted_iota(jnp.int32, (16, 128), 0)
    odd = jnp.where(((row1 >= 4) & (row1 < 8)) | (row1 >= 12), 1, 0)
    src8 = (odd * 4 + seg16).astype(F32)
    ti = lax.broadcasted_iota(jnp.int32, (128, 128), 0)
    tj = lax.broadcasted_iota(jnp.int32, (128, 128), 1)
    start_j = sum(jnp.where(tj >= 32 * a, 32, 0) for a in (1, 2, 3))
    before = jnp.where((ti < tj) & (ti >= start_j), 1.0, 0.0).astype(BF)
    iota_q = lax.broadcasted_iota(jnp.int32, (80, 128), 0).astype(F32)
    iota_k = lax.broadcasted_iota(jnp.int32, (128, 320), 1).astype(F32)

    for r in range(3):
        a_ax, b_ax, c_ax = axes(r, g)
        for k in (1, 2, 3):
            info_b(r, k).wait_recv()
        hits, weights = [], []
        for pair in range(4):
            h, first = pair // 2, pair % 2 * 2
            from_a = [
                2 * (s % 2) + lax.rem(h + first + s // 2 + coord(c_ax), 2) for s in range(4)
            ]
            dest = sum(jnp.where(seg_mask[s], IB[r, first + s // 2, from_a[s], 0:8, :], 0.0) for s in range(4))
            wts = sum(jnp.where(seg_mask[s], IB[r, first + s // 2, from_a[s], 8:16, :], 0.0) for s in range(4))
            for d in range(4):
                target = (dev + (d - coord(c_ax)) * stride(c_ax)).astype(F32)
                hit = dest == target
                hits.append(jnp.sum(jnp.where(hit, 1.0, 0.0), axis=0, keepdims=True))
                weights.append(jnp.sum(jnp.where(hit, wts, 0.0), axis=0, keepdims=True))
        hits = jnp.concatenate(hits, axis=0)
        weights = jnp.concatenate(weights, axis=0)
        rank = dot(hits.astype(BF), before)
        place = jnp.where(rank < MAIN, src8 * MAIN + rank, 64 + src8 * REST + (rank - MAIN))
        place = jnp.where(hits > 0, place, -1000.0)
        fill = jnp.zeros((112, 128), F32)
        place_t = jnp.transpose(jnp.concatenate([place, fill], axis=0))
        weights_t = jnp.transpose(jnp.concatenate([weights, fill], axis=0))
        for pair in range(4):
            total = jnp.zeros((128, 320), F32)
            cols = slice(pair % 2 * 128, pair % 2 * 128 + 128)
            for d in range(4):
                at = pair * 4 + d
                SEL[r, pair // 2, d * 80 : d * 80 + 80, cols] = jnp.where(
                    iota_q == place[at : at + 1, :], 1.0, 0.0
                ).astype(BF)
                total = total + jnp.where(
                    iota_k == place_t[:, at : at + 1] + 80.0 * d, weights_t[:, at : at + 1], 0.0
                )
            WT[r, pair // 2, cols, :] = total.astype(BF)

    def select(i, h):
        r = lax.rem(i, 3)
        a, b, c = axes(r, g)
        for k in (1, 3):
            b_on(i, h, k).wait_recv()
        SB[i, h] = dot(SEL[r, h], B[i, h]).astype(BF).reshape(4, 80, CW)
        for k in (1, 2, 3):
            c_out(i, h, k).start()
        X[i, h, coord(c)] = SB[i, h, coord(c)]

    def multiply(rows_ref, i, h, core):
        rho, _, _ = axes(lax.rem(i, 3), core)
        rows = rows_ref[i, h].reshape(320, CW)
        depth = pl.ds(pl.multiple_of(core * half + i * CW, CW), CW)
        for w, weight in enumerate((WG, WU)):
            acc[w, rho, h * 320 : h * 320 + 320, :] += dot(rows, weight[depth, :])

    def arrived(i, h):
        rho, _, _ = axes(lax.rem(i, 3), g)
        for k in (1, 2, 3):
            c_out(i, h, k).wait_recv()
        rest = jnp.concatenate([X[i, h, c, 64:80, :] for c in range(4)], axis=0)
        rest = dot(perm[0, rho, h], rest).astype(BF)
        for c in range(4):
            X[i, h, c, 64:80, :] = rest[c * 16 : c * 16 + 16, :]
        rows_across(i, h).start()
        multiply(X, i, h, g)

    def crossed(i, h):
        rows_across(i, h).wait_recv()
        multiply(XP, i, h, 1 - g)

    def swiglu(gate, up):
        return gate / (1.0 + jnp.exp(-gate)) * up

    def hidden(h):
        own = [q for q in np.ndindex(4, 4, 4) if sum(q) % 2 == h]
        for q in own:
            rows = [slice(main_row(q, rho), main_row(q, rho) + MAIN) for rho in range(3)]
            gate = acc[0, 0, rows[0], :] + acc[0, 1, rows[1], :] + acc[0, 2, rows[2], :]
            up = acc[1, 0, rows[0], :] + acc[1, 1, rows[1], :] + acc[1, 2, rows[2], :]
            acc[0, 0, rows[0], :] = swiglu(gate, up)
        rest_at = [(h * 4 + c) * 80 + 64 for c in range(4)]
        for at in rest_at:
            rows = slice(at, at + 16)
            gate = acc[0, 0, rows, :] + acc[0, 1, rows, :] + acc[0, 2, rows, :]
            up = acc[1, 0, rows, :] + acc[1, 1, rows, :] + acc[1, 2, rows, :]
            acc[0, 0, rows, :] = swiglu(gate, up)

        rest = jnp.concatenate([acc[0, 0, at : at + 16, :] for at in rest_at], axis=0).astype(BF)
        for rho in range(3):
            for q in own:
                if q[rho] >= 2:
                    continue
                two = list(q)
                two[rho] += 2
                here = main_row(q, rho)
                one, other = main_row(q, 0), main_row(two, 0)
                HR[rho, g, here : here + 16, :] = jnp.concatenate(
                    [acc[0, 0, one : one + MAIN, :], acc[0, 0, other : other + MAIN, :]], axis=0
                ).astype(BF)
            turned = dot(perm[1, rho, h], rest).astype(BF)
            for c in range(4):
                HR[rho, g, rest_at[c] : rest_at[c] + 16, :] = turned[c * 16 : c * 16 + 16, :]
        for r in range(3):
            hidden_across(lax.rem(r + 1 - g, 3), h).start()

    def down(i, h):
        rho, _, c = axes(lax.rem(i, 3), g)
        for k in (1, 2, 3):
            c_out(i, h, k).wait_send()

        @pl.when(i < 3)
        def _():
            hidden_across(rho, h).wait_recv()

        rows = slice(h * 320, h * 320 + 320)
        cols = block(i, CW)
        both = jnp.concatenate([HR[rho, 0, rows, :], HR[rho, 1, rows, :]], axis=1)
        SB[i, h] = dot(both, WD[:, cols]).astype(BF).reshape(4, 80, CW)
        for k in (1, 2, 3):
            c_back(i, h, k).start()
        RB[i, h, coord(c)] = SB[i, h, coord(c)]

    def combine(i, h):
        r = lax.rem(i, 3)
        for k in (1, 2, 3):
            c_back(i, h, k).wait_recv()
        for k in (1, 3):
            b_ag(i, h, k).wait_send()
            b_on(i, h, k).wait_send()
        rows = RB[i, h].reshape(320, CW)
        B[i, h] = dot(WT[r, h], rows).astype(BF)
        for k in (1, 2, 3):
            b_rs(i, h, k).start()

    def first_axis(i, h):
        a, b, c = axes(lax.rem(i, 3), g)
        for k in (1, 2, 3):
            b_rs(i, h, k).wait_recv()
        total = B[i, h, block(coord(b), 64), :].astype(F32)
        for k in range(3):
            total = total + RSB[i, h, k].astype(F32)
        QB[i, h] = total.astype(BF)
        in_half(h, [lambda: a_rs(i, 2).start()], [lambda: a_rs(i, 1).start(), lambda: a_rs(i, 3).start()])

    def finish(i):
        a, b, c = axes(lax.rem(i, 3), g)
        for k in (1, 2, 3):
            a_rs(i, k).wait_recv()
        total = QB[i, parity, block(lax.div(coord(a), 2), 32), :].astype(F32)
        for k in range(3):
            total = total + RA[i, k].astype(F32)
        out[:, block(i, CW)] = total.astype(BF)

    stages((of(pass_on, 1), 0))
    stages((of(select, 0), 0))
    stages((of(select, 1), 0))
    wg_copy.wait()
    wu_copy.wait()
    stages((of(arrived, 0), 0), (of(crossed, 0), 1))
    hidden(0)
    wd_copy.wait()
    wd_across.wait()
    loop(0, EARLY, of(arrived, 1))
    stages((of(down, 0), 0))
    stages((of(arrived, 1), 0, EARLY), (of(crossed, 1), 1), (of(combine, 0), COMBINE))
    hidden(1)
    stages((of(down, 1), 0), (of(first_axis, 0), FIRST), (of(combine, 1), PACE[0]), (of(first_axis, 1), PACE[1]), (finish, PACE[2]))

    @every
    def _(i):
        for k in (1, 2, 3):
            a_ag(i, k).wait_send()
            a_rs(i, k).wait_send()
            for h in range(2):
                c_back(i, h, k).wait_send()
        for k in (1, 2, 3):
            for h in range(2):
                b_rs(i, h, k).wait_send()
        for h in range(2):
            rows_across(i, h).wait_send()

    for r in range(3):
        for k in (1, 2, 3):
            info_a(r, k).wait_send()
            info_b(r, k).wait_send()
        for h in range(2):
            hidden_across(r, h).wait_send()


def body(tokens, routes, route_weights, placement, w_gate, w_up, w_down):
    local_tokens, half = tokens.shape
    n = half // CW
    hid = w_gate.shape[2]
    perm = jnp.asarray(rest_matrices(), BF)
    vmem = pl.BlockSpec(memory_space=pltpu.VMEM)
    hbm = pl.BlockSpec(memory_space=pl.ANY)
    dma = pltpu.SemaphoreType.DMA
    return pl.pallas_call(
        kernel,
        out_shape=jax.ShapeDtypeStruct(tokens.shape, BF),
        in_specs=[vmem, vmem, vmem, pl.BlockSpec(memory_space=pltpu.SMEM), vmem, hbm, hbm, hbm],
        out_specs=vmem,
        scratch_shapes=[
            pltpu.VMEM((2 * half, hid), BF),
            pltpu.VMEM((2 * half, hid), BF),
            pltpu.VMEM((2 * hid, half), BF),
            pltpu.VMEM((n, 2, 256, CW), BF),
            pltpu.VMEM((n, 2, 4, 80, CW), BF),
            pltpu.VMEM((n, 2, 4, 80, CW), BF),
            pltpu.VMEM((n, 2, 4, 80, CW), BF),
            pltpu.VMEM((2, 3, 640, hid), F32),
            pltpu.VMEM((3, 2, 640, hid), BF),
            pltpu.VMEM((n, 2, 4, 80, CW), BF),
            pltpu.VMEM((n, 2, 3, 64, CW), BF),
            pltpu.VMEM((n, 3, 32, CW), BF),
            pltpu.VMEM((n, 2, 64, CW), BF),
            pltpu.VMEM((3, 4, 4, 16, 128), F32),
            pltpu.VMEM((3, 2, 320, 256), BF),
            pltpu.VMEM((3, 2, 256, 320), BF),
            pltpu.VMEM((16, 128), F32),
            dma((7, n, 2, 3)),
            dma((7, n, 2, 3)),
            dma((2, 3, 3)),
            dma((2, 3, 3)),
            dma((n, 2)),
            dma((n, 2)),
            dma((3, 2)),
            dma((3, 2)),
            dma((3,)),
            dma,
            dma,
        ],
        compiler_params=pltpu.CompilerParams(
            collective_id=0, has_side_effects=True, vmem_limit_bytes=64 * 1024 * 1024 - 512 * 1024
        ),
    )(tokens, routes.T, route_weights.T, placement, perm, w_gate, w_up, w_down)


def solution(mesh):
    in_specs = (
        P("dev", "group"),
        P("dev", None),
        P("dev", None),
        P(),
        P("dev", None, "group"),
        P("dev", None, "group"),
        P("dev", "group", None),
    )
    out_specs = P("dev", "group")
    return jax.shard_map(body, mesh=mesh, in_specs=in_specs, out_specs=out_specs, check_vma=False)
```

time: 110 us -> 93.5 us (0.85)
  the two profiles are of different devices: /device:TPU:1 before, /device:TPU:32 now
where the time goes in v2:
time: 93.5 us; the launch traced here: 93.3 us
  Pallas kernels  91.7 us (98%)
  local copies, waits for them, and re-layouts  1.64 us (2%)
    pallas_call x1, Pallas kernels, body(): pl.pallas_call(kernel, out_shape=jax.ShapeDtypeStruct(tokens.shape, BF),...  91.7 us

profile of v2, /device:TPU:32, one launch (start us, length us, event | category | flops | bytes accessed | tf_op | source)
XLA Modules:
  0.0 93.3 jit_solution(6825447423160483194)
XLA Ops:
  0.0 91.7 %shard_map.82 = bf16[32,3584]{1,0:T(8,128)(2,1)} custom-call(bf16[32,3584]{1,0:T(8,128)(2,1)} %tok.1, s32[8,32]{1,0:T(8,128)} %bitcast.2, f32[8,32]{1,0:T(8,128)} %bitcast.3, s32[64]{0:T(128)} %placement.1, bf16[2,3,2,64,64]{4,3,2,1,0:T(8,128)(2,1)} %constant.2.clone.perm, bf16[1,7168,512]{2,1,0:T(8,128)(2,1)} %wg_hbm.1, bf16[1,7168,512]{2,1,0:T(8,128)(2,1)} %wu_hbm.1, ...), custom_call_target="tpu_custom_call" | custom-call | tf_op jit(solution)/shard_map/pallas_call | solution.py:440
  91.7 1.6 %copy.10 = bf16[32,3584]{1,0:T(8,128)(2,1)} copy(bf16[32,3584]{1,0:T(8,128)(2,1)} %shard_map.82) | data formatting | bytes 458752

commit v3 on v2

--- a/solution.py
+++ b/solution.py
@@ -12,8 +12,9 @@
 CW = 512
 EARLY = 2
 COMBINE = 3
-FIRST = 5
-PACE = (5, 9, 12)
+FIRST = 6
+SPLIT = 5
+PACE = (6, 10, 13)
 MAIN, REST = 8, 2
 A_AG, B_AG, B_ON, C_OUT, C_BACK, B_RS, A_RS = range(7)
 
@@ -54,19 +55,25 @@
     n = B.shape[0]
     half = n * CW
 
+    place = (lax.div(dev, 16), lax.rem(lax.div(dev, 4), 4), lax.rem(dev, 4))
+
+    def one_of(ax, first, second, third):
+        return jnp.where(ax == 0, first, jnp.where(ax == 1, second, third))
+
     def stride(ax):
-        return lax.div(32 - 33 * ax + 9 * ax * ax, 2)
+        return one_of(ax, 16, 4, 1)
 
     def coord(ax):
-        return lax.rem(lax.div(dev, stride(ax)), 4)
+        return one_of(ax, *place)
 
     def peer(ax, k):
         at = coord(ax)
         return dev + (lax.rem(at + k, 4) - at) * stride(ax)
 
     def axes(slot, core):
-        rho = lax.rem(slot + core, 3)
-        return rho, lax.rem(rho + 2, 3), lax.rem(rho + 1, 3)
+        rho = slot + core
+        rho = jnp.where(rho == 3, 0, rho)
+        return rho, jnp.where(rho == 0, 2, rho - 1), jnp.where(rho == 2, 0, rho + 1)
 
     def remote(src, dst, s, r, ax, k):
         return pltpu.make_async_remote_copy(
@@ -81,66 +88,71 @@
     def block(i, size):
         return pl.ds(pl.multiple_of(i * size, size), size)
 
-    parity = lax.rem(coord(0) + coord(1) + coord(2), 2)
+    parity = lax.rem(place[0] + place[1] + place[2], 2)
 
     def a_ag(i, k):
         a, b, c = axes(lax.rem(i, 3), g)
         here = B.at[i, parity, block(coord(b) * 2 + lax.div(coord(a), 2), 32)]
-        sems = (A_AG, i, 0, k - 1)
-        return remote(tok.at[:, block(i, CW)], here, ss.at[sems], rs.at[sems], a, k)
+        return remote(tok.at[:, block(i, CW)], here, ss.at[A_AG, 0], rs.at[A_AG, i, parity], a, k)
 
     def b_ag(i, h, k):
         a, b, c = axes(lax.rem(i, 3), g)
         here = B.at[i, h, block(coord(b), 64)]
-        sems = (B_AG, i, h, k - 1)
-        return remote(here, here, ss.at[sems], rs.at[sems], b, k)
+        sems = ss.at[B_AG, h], rs.at[B_AG, i, h]
+        return remote(here, here, *sems, b, k)
 
     def b_on(i, h, k):
         a, b, c = axes(lax.rem(i, 3), g)
         here = B.at[i, h, block(lax.rem(coord(b) + 4 - k, 4) * 2 + (k - 1) // 2, 32)]
-        sems = (B_ON, i, h, k - 1)
-        return remote(here, here, ss.at[sems], rs.at[sems], b, k)
+        sems = ss.at[B_ON, h], rs.at[B_ON, i, h]
+        return remote(here, here, *sems, b, k)
 
     def c_out(i, h, k):
         a, b, c = axes(lax.rem(i, 3), g)
         to = lax.rem(coord(c) + k, 4)
-        sems = (C_OUT, i, h, k - 1)
-        return remote(SB.at[i, h, to], X.at[i, h, coord(c)], ss.at[sems], rs.at[sems], c, k)
+        sems = ss.at[C_OUT, h], rs.at[C_OUT, i, h]
+        return remote(SB.at[i, h, to], X.at[i, h, coord(c)], *sems, c, k)
 
     def c_back(i, h, k):
         a, b, c = axes(lax.rem(i, 3), g)
         to = lax.rem(coord(c) + k, 4)
-        sems = (C_BACK, i, h, k - 1)
-        return remote(SB.at[i, h, to], RB.at[i, h, coord(c)], ss.at[sems], rs.at[sems], c, k)
+        sems = ss.at[C_BACK, h], rs.at[C_BACK, i, h]
+        return remote(SB.at[i, h, to], RB.at[i, h, coord(c)], *sems, c, k)
 
     def b_rs(i, h, k):
         a, b, c = axes(lax.rem(i, 3), g)
         to = lax.rem(coord(b) + k, 4)
-        sems = (B_RS, i, h, k - 1)
-        return remote(B.at[i, h, block(to, 64)], RSB.at[i, h, k - 1], ss.at[sems], rs.at[sems], b, k)
+        sems = ss.at[B_RS, h], rs.at[B_RS, i, h]
+        return remote(B.at[i, h, block(to, 64)], RSB.at[i, h, k - 1], *sems, b, k)
 
     def a_rs(i, k):
         a, b, c = axes(lax.rem(i, 3), g)
         to = lax.div(lax.rem(coord(a) + k, 4), 2)
         h = parity if k == 2 else 1 - parity
-        sems = (A_RS, i, 0, k - 1)
-        return remote(QB.at[i, h, block(to, 32)], RA.at[i, k - 1], ss.at[sems], rs.at[sems], a, k)
+        sems = ss.at[A_RS, 0], rs.at[A_RS, i, 0]
+        return remote(QB.at[i, h, block(to, 32)], RA.at[i, k - 1], *sems, a, k)
 
     def info_a(r, k):
         a, b, c = axes(r, g)
-        return remote(info, IB.at[r, coord(b), coord(a)], iss.at[0, r, k - 1], irs.at[0, r, k - 1], a, k)
+        return remote(info, IB.at[r, coord(b), coord(a)], iss.at[0], irs.at[0, r], a, k)
 
     def info_b(r, k):
         a, b, c = axes(r, g)
         here = IB.at[r, coord(b)]
-        return remote(here, here, iss.at[1, r, k - 1], irs.at[1, r, k - 1], b, k)
+        return remote(here, here, iss.at[1], irs.at[1, r], b, k)
 
     def rows_across(i, h):
-        return across(X.at[i, h], XP.at[i, h], ess.at[i, h], ers.at[i, h])
+        return across(X.at[i, h], XP.at[i, h], ess, ers.at[i, h])
 
     def hidden_across(rho, h):
         part = HR.at[rho, g, pl.ds(h * 320, 320)]
-        return across(part, part, hss.at[rho, h], hrs.at[rho, h])
+        return across(part, part, hss, hrs.at[rho, h])
+
+    def landed(all_of, sem):
+        across(all_of, all_of, sem, sem).wait_recv()
+
+    def sent(all_of, sem):
+        across(all_of, all_of, sem, sem).wait_send()
 
     def in_half(h, same, other):
         pl.when(parity == h)(lambda: [fn() for fn in same] and None)
@@ -161,11 +173,11 @@
 
     def stages(*work):
         def step(s):
-            for fn, lag, *first in work:
-                start = lag + (first[0] if first else 0)
-                pl.when((s >= start) & (s < n + lag))(lambda fn=fn, lag=lag: fn(s - lag))
-
-        loop(0, n + max(w[1] for w in work), step)
+            for fn, lag, *span in work:
+                first, last = span or (0, n)
+                pl.when((s >= first + lag) & (s < last + lag))(lambda fn=fn, lag=lag: fn(s - lag))
+
+        loop(0, max(lag + (span[1] if span else n) for _, lag, *span in work), step)
 
     bar = pltpu.get_barrier_semaphore()
     for ax in range(3):
@@ -177,7 +189,6 @@
         dest = jnp.where(routes[...] == e, placement[e], dest)
     info[0:8, :] = jnp.concatenate([dest.astype(F32)] * 4, axis=1)
     info[8:16, :] = jnp.concatenate([weights_in[...]] * 4, axis=1)
-    acc[...] = jnp.zeros_like(acc)
     pl.semaphore_wait(bar, 10)
 
     for r in range(3):
@@ -206,25 +217,26 @@
     def second_axis(i, h):
         in_half(
             h,
-            [lambda: a_ag(i, 2).wait_recv()],
-            [lambda: a_ag(i, 1).wait_recv(), lambda: a_ag(i, 3).wait_recv()],
+            [lambda: landed(B.at[i, h, 0:32], rs.at[A_AG, i, h])],
+            [lambda: landed(B.at[i, h, 0:64], rs.at[A_AG, i, h])],
         )
         for k in (1, 3):
             b_ag(i, h, k).start()
 
     def pass_on(i, h):
+        landed(B.at[i, h, 0:128], rs.at[B_AG, i, h])
         for k in (1, 3):
-            b_ag(i, h, k).wait_recv()
             b_on(i, h, k).start()
 
     for r in range(3):
-        for k in (1, 2, 3):
-            info_a(r, k).wait_recv()
+        landed(IB.at[r, 0, 0:3], irs.at[0, r])
         for k in (1, 2, 3):
             info_b(r, k).start()
 
     stages((of(second_axis, 0), 0))
     stages((of(second_axis, 1), 0), (of(pass_on, 0), 0))
+
+    acc[...] = jnp.zeros_like(acc)
 
     lane = lax.broadcasted_iota(jnp.int32, (8, 128), 1)
     seg_mask = [(lane >= 32 * a) & (lane < 32 * a + 32) for a in range(4)]
@@ -242,8 +254,7 @@
 
     for r in range(3):
         a_ax, b_ax, c_ax = axes(r, g)
-        for k in (1, 2, 3):
-            info_b(r, k).wait_recv()
+        landed(IB.at[r, 0:3], irs.at[1, r])
         hits, weights = [], []
         for pair in range(4):
             h, first = pair // 2, pair % 2 * 2
@@ -260,10 +271,10 @@
         hits = jnp.concatenate(hits, axis=0)
         weights = jnp.concatenate(weights, axis=0)
         rank = dot(hits.astype(BF), before)
-        place = jnp.where(rank < MAIN, src8 * MAIN + rank, 64 + src8 * REST + (rank - MAIN))
-        place = jnp.where(hits > 0, place, -1000.0)
+        at_row = jnp.where(rank < MAIN, src8 * MAIN + rank, 64 + src8 * REST + (rank - MAIN))
+        at_row = jnp.where(hits > 0, at_row, -1000.0)
         fill = jnp.zeros((112, 128), F32)
-        place_t = jnp.transpose(jnp.concatenate([place, fill], axis=0))
+        place_t = jnp.transpose(jnp.concatenate([at_row, fill], axis=0))
         weights_t = jnp.transpose(jnp.concatenate([weights, fill], axis=0))
         for pair in range(4):
             total = jnp.zeros((128, 320), F32)
@@ -271,7 +282,7 @@
             for d in range(4):
                 at = pair * 4 + d
                 SEL[r, pair // 2, d * 80 : d * 80 + 80, cols] = jnp.where(
-                    iota_q == place[at : at + 1, :], 1.0, 0.0
+                    iota_q == at_row[at : at + 1, :], 1.0, 0.0
                 ).astype(BF)
                 total = total + jnp.where(
                     iota_k == place_t[:, at : at + 1] + 80.0 * d, weights_t[:, at : at + 1], 0.0
@@ -281,8 +292,7 @@
     def select(i, h):
         r = lax.rem(i, 3)
         a, b, c = axes(r, g)
-        for k in (1, 3):
-            b_on(i, h, k).wait_recv()
+        landed(B.at[i, h, 0:64], rs.at[B_ON, i, h])
         SB[i, h] = dot(SEL[r, h], B[i, h]).astype(BF).reshape(4, 80, CW)
         for k in (1, 2, 3):
             c_out(i, h, k).start()
@@ -297,8 +307,7 @@
 
     def arrived(i, h):
         rho, _, _ = axes(lax.rem(i, 3), g)
-        for k in (1, 2, 3):
-            c_out(i, h, k).wait_recv()
+        landed(X.at[i, h, 0:3], rs.at[C_OUT, i, h])
         rest = jnp.concatenate([X[i, h, c, 64:80, :] for c in range(4)], axis=0)
         rest = dot(perm[0, rho, h], rest).astype(BF)
         for c in range(4):
@@ -347,8 +356,6 @@
 
     def down(i, h):
         rho, _, c = axes(lax.rem(i, 3), g)
-        for k in (1, 2, 3):
-            c_out(i, h, k).wait_send()
 
         @pl.when(i < 3)
         def _():
@@ -364,11 +371,7 @@
 
     def combine(i, h):
         r = lax.rem(i, 3)
-        for k in (1, 2, 3):
-            c_back(i, h, k).wait_recv()
-        for k in (1, 3):
-            b_ag(i, h, k).wait_send()
-            b_on(i, h, k).wait_send()
+        landed(RB.at[i, h, 0:3], rs.at[C_BACK, i, h])
         rows = RB[i, h].reshape(320, CW)
         B[i, h] = dot(WT[r, h], rows).astype(BF)
         for k in (1, 2, 3):
@@ -376,8 +379,7 @@
 
     def first_axis(i, h):
         a, b, c = axes(lax.rem(i, 3), g)
-        for k in (1, 2, 3):
-            b_rs(i, h, k).wait_recv()
+        landed(RSB.at[i, h], rs.at[B_RS, i, h])
         total = B[i, h, block(coord(b), 64), :].astype(F32)
         for k in range(3):
             total = total + RSB[i, h, k].astype(F32)
@@ -386,8 +388,7 @@
 
     def finish(i):
         a, b, c = axes(lax.rem(i, 3), g)
-        for k in (1, 2, 3):
-            a_rs(i, k).wait_recv()
+        landed(RA.at[i], rs.at[A_RS, i, 0])
         total = QB[i, parity, block(lax.div(coord(a), 2), 32), :].astype(F32)
         for k in range(3):
             total = total + RA[i, k].astype(F32)
@@ -403,30 +404,26 @@
     wd_copy.wait()
     wd_across.wait()
     loop(0, EARLY, of(arrived, 1))
+    sent(X.at[:, 0, 0:3], ss.at[C_OUT, 0])
     stages((of(down, 0), 0))
-    stages((of(arrived, 1), 0, EARLY), (of(crossed, 1), 1), (of(combine, 0), COMBINE))
+    for h in range(2):
+        sent(B.at[:, h, 0:128], ss.at[B_AG, h])
+        sent(B.at[:, h, 0:64], ss.at[B_ON, h])
+    stages((of(arrived, 1), 0, EARLY, n), (of(crossed, 1), 1), (of(combine, 0), COMBINE, 0, SPLIT))
     hidden(1)
+    loop(SPLIT, n, of(combine, 0))
+    sent(X.at[:, 1, 0:3], ss.at[C_OUT, 1])
     stages((of(down, 1), 0), (of(first_axis, 0), FIRST), (of(combine, 1), PACE[0]), (of(first_axis, 1), PACE[1]), (finish, PACE[2]))
 
-    @every
-    def _(i):
-        for k in (1, 2, 3):
-            a_ag(i, k).wait_send()
-            a_rs(i, k).wait_send()
-            for h in range(2):
-                c_back(i, h, k).wait_send()
-        for k in (1, 2, 3):
-            for h in range(2):
-                b_rs(i, h, k).wait_send()
-        for h in range(2):
-            rows_across(i, h).wait_send()
-
-    for r in range(3):
-        for k in (1, 2, 3):
-            info_a(r, k).wait_send()
-            info_b(r, k).wait_send()
-        for h in range(2):
-            hidden_across(r, h).wait_send()
+    sent(B.at[:, 0, 0:96], ss.at[A_AG, 0])
+    for h in range(2):
+        sent(RB.at[:, h, 0:3], ss.at[C_BACK, h])
+        sent(RSB.at[:, h], ss.at[B_RS, h])
+    sent(RA, ss.at[A_RS, 0])
+    sent(XP, ess)
+    sent(HR.at[:, 0], hss)
+    sent(IB.at[:, 0, 0:3], iss.at[0])
+    sent(IB.at[:, 0:3], iss.at[1])
 
 
 def body(tokens, routes, route_weights, placement, w_gate, w_up, w_down):
@@ -460,13 +457,13 @@
             pltpu.VMEM((3, 2, 320, 256), BF),
             pltpu.VMEM((3, 2, 256, 320), BF),
             pltpu.VMEM((16, 128), F32),
-            dma((7, n, 2, 3)),
-            dma((7, n, 2, 3)),
-            dma((2, 3, 3)),
-            dma((2, 3, 3)),
+            dma((7, 2)),
+            dma((7, n, 2)),
+            dma((2,)),
+            dma((2, 3)),
+            dma,
             dma((n, 2)),
-            dma((n, 2)),
-            dma((3, 2)),
+            dma,
             dma((3, 2)),
             dma((3,)),
             dma,

time: 93.5 us -> 87.9 us (0.940)
  the two profiles are of different devices: /device:TPU:32 before, /device:TPU:1 now
where the time goes in v3:
time: 87.9 us; the launch traced here: 86.4 us
  Pallas kernels  84.8 us (96%)
  local copies, waits for them, and re-layouts  1.64 us (2%)
    pallas_call x1, Pallas kernels, body(): pl.pallas_call(kernel, out_shape=jax.ShapeDtypeStruct(tokens.shape, BF),...  84.8 us

profile of v3, /device:TPU:1, one launch (start us, length us, event | category | flops | bytes accessed | tf_op | source)
XLA Modules:
  0.0 86.4 jit_solution(12748153347507055654)
XLA Ops:
  0.0 84.8 %shard_map.82 = bf16[32,3584]{1,0:T(8,128)(2,1)} custom-call(bf16[32,3584]{1,0:T(8,128)(2,1)} %tok.1, s32[8,32]{1,0:T(8,128)} %bitcast.2, f32[8,32]{1,0:T(8,128)} %bitcast.3, s32[64]{0:T(128)} %placement.1, bf16[2,3,2,64,64]{4,3,2,1,0:T(8,128)(2,1)} %constant.2.clone.perm, bf16[1,7168,512]{2,1,0:T(8,128)(2,1)} %wg_hbm.1, bf16[1,7168,512]{2,1,0:T(8,128)(2,1)} %wu_hbm.1, ...), custom_call_target="tpu_custom_call" | custom-call | tf_op jit(solution)/shard_map/pallas_call | solution.py:437
  84.8 1.6 %copy.10 = bf16[32,3584]{1,0:T(8,128)(2,1)} copy(bf16[32,3584]{1,0:T(8,128)(2,1)} %shard_map.82) | data formatting | bytes 458752

commit v4 on v3

--- a/solution.py
+++ b/solution.py
@@ -12,9 +12,9 @@
 CW = 512
 EARLY = 2
 COMBINE = 3
-FIRST = 6
+FIRST = 7
 SPLIT = 5
-PACE = (6, 10, 13)
+PACE = (7, 11, 14)
 MAIN, REST = 8, 2
 A_AG, B_AG, B_ON, C_OUT, C_BACK, B_RS, A_RS = range(7)
 

time: 87.9 us -> 87.9 us (level)
  no operation moved by 1% of the time
where the time goes in v4:
time: 87.9 us; the launch traced here: 86.4 us
  Pallas kernels  84.8 us (96%)
  local copies, waits for them, and re-layouts  1.64 us (2%)
    pallas_call x1, Pallas kernels, body(): pl.pallas_call(kernel, out_shape=jax.ShapeDtypeStruct(tokens.shape, BF),...  84.8 us

profile of v4, /device:TPU:1, one launch (start us, length us, event | category | flops | bytes accessed | tf_op | source)
XLA Modules:
  0.0 86.4 jit_solution(1747664330987122401)
XLA Ops:
  0.0 84.8 %shard_map.82 = bf16[32,3584]{1,0:T(8,128)(2,1)} custom-call(bf16[32,3584]{1,0:T(8,128)(2,1)} %tok.1, s32[8,32]{1,0:T(8,128)} %bitcast.2, f32[8,32]{1,0:T(8,128)} %bitcast.3, s32[64]{0:T(128)} %placement.1, bf16[2,3,2,64,64]{4,3,2,1,0:T(8,128)(2,1)} %constant.2.clone.perm, bf16[1,7168,512]{2,1,0:T(8,128)(2,1)} %wg_hbm.1, bf16[1,7168,512]{2,1,0:T(8,128)(2,1)} %wu_hbm.1, ...), custom_call_target="tpu_custom_call" | custom-call | tf_op jit(solution)/shard_map/pallas_call | solution.py:437
  84.8 1.6 %copy.10 = bf16[32,3584]{1,0:T(8,128)(2,1)} copy(bf16[32,3584]{1,0:T(8,128)(2,1)} %shard_map.82) | data formatting | bytes 458752
